TPU v7x, 256 devices: a whole 4x4x8 slice. The times are simulated.
256 devices in a mesh: section: 2 (over y_lo), fsdp: 32 (over x, z), dp: 4 (over y_hi, core).
Axes of the slice: x: 4, y: 4 (y_hi: 2, y_lo: 2; y = y_hi * 2 + y_lo), z: 8, core: 2. Of those that a mesh axis runs over, the one named last changes fastest.
Arguments:
- activations: bfloat16 [2, 4, 4096, 3584], P('section', None, ('fsdp', 'dp')), may hold values from -6 to 6
- out_grad: bfloat16 [2, 4, 4096, 14336], P('section', None, ('fsdp', 'dp')), may hold values from -6 to 6
- blocks: bfloat16 [2, 128, 128, 128], P('section', 'fsdp'), may hold values from -0.5 to 0.5
- pattern: int32 [2, 128, 2], P('section', 'fsdp'), may hold values from 0 to 111, as said below
- order: int32 [4], replicated, may hold values from 0 to 3, each once
Outputs:
- received: bfloat16 [2, 4, 4096, 3584], P('section', None, ('fsdp', 'dp'))
- weight_grad: float32 [2, 128, 128, 128], P('section', 'fsdp')
Inputs may be any that keep to these rules, and one draw needn't show every extreme that they name: pattern[s, b, 0] < 28 and pattern[s, b, 1] < 112; no two blocks of one section share both indices; within a section the blocks stand in ascending order of (row, column). `order`: a permutation of the microbatches.
All inputs are finite; a program needn't handle non-finite values.
Results may differ from a plain program's by a relative error of at most 0.0049.
Values may be sent and summed in bfloat16 or wider, within the bound.
A program may use at most 128 MiB of HBM per device.

v0:
```python
import math
import jax
import jax.numpy as jnp
from jax import lax
from jax.sharding import PartitionSpec as P


def passed_along(block, axis, distance):
    devices = range(lax.axis_size(axis))
    route = [(i - distance, i) for i in devices if i - distance in devices]
    return lax.ppermute(block, axis, route)


def silu_slope(pre_act):
    sigmoid_val = jax.nn.sigmoid(pre_act)
    return sigmoid_val * (1.0 + pre_act * (1.0 - sigmoid_val))


def in_groups(step_fn, running, shard_blocks):
    block_count = shard_blocks.shape[0]
    group_size = math.gcd(block_count, 32)

    def one_group(number, carried):
        segment = lax.dynamic_slice_in_dim(shard_blocks, number * group_size, group_size, 0)
        return step_fn(carried, segment, number * group_size)

    return lax.fori_loop(0, block_count // group_size, one_group, running)


def local(activations, out_grad, blocks, pattern, order):
    block_size = blocks.shape[-1]
    micro_count = activations.shape[1]
    tok_rows = activations.shape[1] * activations.shape[2]
    row_count = activations.shape[3] // block_size
    col_count = out_grad.shape[3] // block_size
    features = activations[0].reshape(tok_rows, row_count, block_size)
    hidden_grad = out_grad[0].reshape(tok_rows, out_grad.shape[3])
    own_blocks = blocks[0]
    all_indices = lax.all_gather(pattern[0], "fsdp", axis=0, tiled=True)

    def forward_step(running, shard_blocks, first_block):
        indices = lax.dynamic_slice_in_dim(all_indices, first_block, shard_blocks.shape[0], 0)
        rows_in = jnp.take(features, indices[:, 0], axis=1)
        product = jnp.einsum(
            "tbk,bkn->tbn", rows_in, shard_blocks, preferred_element_type=jnp.float32
        )
        return running.at[:, indices[:, 1]].add(product)

    pre_zero = jnp.zeros((tok_rows, col_count, block_size), jnp.float32)
    pre_act = in_groups(
        forward_step, pre_zero, lax.all_gather(own_blocks, "fsdp", axis=0, tiled=True)
    )
    act_grad = (hidden_grad.astype(jnp.float32) * silu_slope(pre_act.reshape(tok_rows, -1))).astype(
        jnp.bfloat16
    )
    grad_cols = act_grad.reshape(tok_rows, col_count, block_size)

    def backward_step(running, shard_blocks, first_block):
        indices = lax.dynamic_slice_in_dim(all_indices, first_block, shard_blocks.shape[0], 0)
        cols_in = jnp.take(grad_cols, indices[:, 1], axis=1)
        product = jnp.einsum(
            "tbn,bkn->tbk", cols_in, shard_blocks, preferred_element_type=jnp.float32
        )
        return running.at[:, indices[:, 0]].add(product)

    back_zero = jnp.zeros((tok_rows, row_count, block_size), jnp.float32)
    input_grad = in_groups(
        backward_step, back_zero, lax.all_gather(own_blocks, "fsdp", axis=0, tiled=True)
    )
    input_grad = input_grad.astype(jnp.bfloat16).reshape(
        micro_count, activations.shape[2], activations.shape[3]
    )
    ordered = jnp.take(input_grad, order, axis=0)
    received = passed_along(ordered, "section", -1)
    indices = all_indices
    rows_in = jnp.take(features, indices[:, 0], axis=1)
    cols_in = jnp.take(grad_cols, indices[:, 1], axis=1)
    owned_grads = lax.psum_scatter(
        jnp.einsum("tbk,tbn->bkn", rows_in, cols_in, preferred_element_type=jnp.float32),
        "fsdp",
        scatter_dimension=0,
        tiled=True,
    )
    summed = lax.psum(owned_grads, "dp")
    grad_scale = 1.0 / math.sqrt(tok_rows * lax.axis_size("fsdp") * lax.axis_size("dp"))
    return (received[None], (summed * grad_scale)[None])


def solution(mesh):
    in_specs = (
        P("section", None, ("fsdp", "dp"), None),
        P("section", None, ("fsdp", "dp"), None),
        P("section", "fsdp", None, None),
        P("section", "fsdp", None),
        P(),
    )
    out_specs = (P("section", None, ("fsdp", "dp"), None), P("section", "fsdp", None, None))
    return jax.shard_map(local, mesh=mesh, in_specs=in_specs, out_specs=out_specs, check_vma=False)
```

profile of v0, /device:TPU:1, one launch (start us, length us, event | category | flops | bytes accessed | tf_op | source)
XLA Modules:
  0.0 444.8 jit_solution(14893785248069533942)
XLA Ops:
  7.2 0.0 all-gather.4.cloned.1.call-start
  7.2 0.7 all-gather.4.cloned.1.call-update
  7.9 0.0 reduce-scatter.2.cloned.1.call-start
  7.9 0.8 copy.31
  8.7 40.7 %all-gather = s32[1,128,2]{2,0,1:T(1,128)S(1)} all-gather(s32[1,4,2]{2,0,1:T(1,128)S(1)} %copy.31), channel_id=2, replica_groups=mesh['section'=2,'fsdp'=32,'dp'=4] {'fsdp'}, dimensions={1}, use_global_device_ids=true | all-gather | bytes 1056 | tf_op jit(solution)/shard_map/all_gather | solution.py:39
  49.4 0.1 copy.36
  49.5 1.6 reshape_squeeze.4
  51.1 0.4 copy.34
  51.5 5.9 %copy.41 = f32[16,8,112,128]{3,2,1,0:T(8,128)} copy(bf16[16,8,112,128]{3,1,2,0:T(8,128)(2,1)} %bitcast.51) | data formatting | bytes 11010048
  57.3 0.2 fusion.29
  57.5 3.1 gather_fusion.3
  60.6 0.2 and_reduce_fusion.1
  60.8 32.7 %all-gather.4.cloned.1.call-done = bf16[1,128,128,128]{3,2,0,1:T(8,128)(2,1)} async-done(((bf16[1,4,128,128]{3,2,0,1:T(8,128)(2,1)}), bf16[1,128,128,128]{3,2,0,1:T(8,128)(2,1)}) %all-gather.4.cloned.1.call-update) | async-done | bytes 4194320 | tf_op jit(solution)/shard_map/all_gather | solution.py:68
  93.5 3.9 broadcast_in_dim.90
  97.5 40.1 %while.26 = (s32[]{:T(128)}, f32[128,112,128]{2,0,1:T(8,128)}, s32[128,2]{0,1:T(2,128)S(1)}, bf16[128,128,128]{2,1,0:T(8,128)(2,1)}, bf16[128,28,128]{2,0,1:T(8,...) while((s32[]{:T(128)}, f32[128,112,128]{2,0,1:T(8,128)}, s32[128,2]{0,1:T(2,128)S(1)}, ...), condition=%wide.region_2.3_spmd, body=%wide.region_0.2_spmd.sunk | while | flops 135267712 | bytes 12588755 | solution.py:27
  97.5 0.1 constant_dynamic-slice_fusion.4
  97.5 1.7 gather_fusion
  99.2 2.0 fusion.43
  101.3 6.2 %scatter_fusion = f32[128,112,128]{2,0,1:T(8,128)} fusion(f32[128,112,128]{2,0,1:T(8,128)} %get-tuple-element.332, s32[32]{0:T(128)S(1)} %get-tuple-element.313, f32[32,128,128]{2,1,0:T(8,128)S(1)} %fusion.43), kind=kCustom, calls=%fused_computation.5.clone.1 | custom fusion | flops 524288 | bytes 6291584 | tf_op jit(solution)/shard_map/while/body/eval_jaxpr/scatter-add | solution.py:47
  107.5 0.1 constant_dynamic-slice_fusion.4
  107.6 1.7 gather_fusion
  109.3 2.0 fusion.43
  111.3 6.2 %scatter_fusion = f32[128,112,128]{2,0,1:T(8,128)} fusion(f32[128,112,128]{2,0,1:T(8,128)} %get-tuple-element.332, s32[32]{0:T(128)S(1)} %get-tuple-element.313, f32[32,128,128]{2,1,0:T(8,128)S(1)} %fusion.43), kind=kCustom, calls=%fused_computation.5.clone.1 | custom fusion | flops 524288 | bytes 6291584 | tf_op jit(solution)/shard_map/while/body/eval_jaxpr/scatter-add | solution.py:47
  117.5 0.1 constant_dynamic-slice_fusion.4
  117.6 1.7 gather_fusion
  119.3 2.0 fusion.43
  121.3 6.2 %scatter_fusion = f32[128,112,128]{2,0,1:T(8,128)} fusion(f32[128,112,128]{2,0,1:T(8,128)} %get-tuple-element.332, s32[32]{0:T(128)S(1)} %get-tuple-element.313, f32[32,128,128]{2,1,0:T(8,128)S(1)} %fusion.43), kind=kCustom, calls=%fused_computation.5.clone.1 | custom fusion | flops 524288 | bytes 6291584 | tf_op jit(solution)/shard_map/while/body/eval_jaxpr/scatter-add | solution.py:47
  127.5 0.1 constant_dynamic-slice_fusion.4
  127.6 1.7 gather_fusion
  129.3 2.0 fusion.43
  131.3 6.2 %scatter_fusion = f32[128,112,128]{2,0,1:T(8,128)} fusion(f32[128,112,128]{2,0,1:T(8,128)} %get-tuple-element.332, s32[32]{0:T(128)S(1)} %get-tuple-element.313, f32[32,128,128]{2,1,0:T(8,128)S(1)} %fusion.43), kind=kCustom, calls=%fused_computation.5.clone.1 | custom fusion | flops 524288 | bytes 6291584 | tf_op jit(solution)/shard_map/while/body/eval_jaxpr/scatter-add | solution.py:47
  137.5 8.5 %fusion.20 = bf16[128,112,128]{2,0,1:T(8,128)(2,1)} fusion(f32[128,112,128]{2,1,0:T(8,128)} %bitcast.49, f32[128,112,128]{2,0,1:T(8,128)} %get-tuple-element.190), kind=kLoop, calls=%fused_computation.38 | loop fusion | flops 16515072 | bytes 18350080 | tf_op jit(solution)/shard_map/convert_element_type | solution.py:53
  146.0 5.1 %gather_fusion.4 = bf16[128,128,128]{2,1,0:T(8,128)(2,1)} fusion(bf16[128,112,128]{2,0,1:T(8,128)(2,1)} %fusion.20, s32[1024]{0:T(1024)S(1)} %get-tuple-element.250), kind=kCustom, calls=%fused_computation.4 | custom fusion | bytes 8389120 | tf_op jit(solution)/shard_map/jit(_take)/gather | solution.py:77
  151.1 8.5 %fusion.21 = f32[128,128,128]{2,1,0:T(8,128)} fusion(bf16[128,128,128]{2,1,0:T(8,128)(2,1)} %gather_fusion.4, bf16[128,128,128]{2,1,0:T(8,128)(2,1)} %gather_fusion.3, pred[128]{0:T(512)(128)(4,1)S(1)} %get-tuple-element.223, pred[128]{0:T(512)(128)(4,1)S(1)} %get-tuple-element.222), kind=kOutput, calls=%fused_computation.39 | convolution fusion | flops 541065216 | bytes 16777472 | tf_op jit(solution)/shard_map/tbk,tbn->bkn/dot_general | solution.py:79
  159.7 0.2 all-reduce.2.cloned.1.call-start
  159.9 0.4 copy-done
  160.3 1.5 broadcast_in_dim.89
  161.8 45.7 %while.27 = (s32[]{:T(128)}, f32[128,28,128]{2,0,1:T(8,128)}, s32[128,2]{0,1:T(2,128)S(1)}, bf16[128,128,128]{2,1,0:T(8,128)(2,1)}, bf16[128,112,128]{2,0,1:T(8,...) while((s32[]{:T(128)}, f32[128,28,128]{2,0,1:T(8,128)}, s32[128,2]{0,1:T(2,128)S(1)}, ...), condition=%wide.region_5.6_spmd, body=%wide.region_3.5_spmd.sunk | while | flops 135267712 | bytes 12588755 | solution.py:27
  161.8 0.1 constant_dynamic-slice_fusion.5
  161.9 2.8 gather_fusion.1
  164.7 2.1 fusion.47
  166.8 6.4 %scatter_fusion.1 = f32[128,28,128]{2,0,1:T(8,128)} fusion(f32[128,28,128]{2,0,1:T(8,128)} %get-tuple-element.359, s32[32]{0:T(128)S(1)} %get-tuple-element.320, f32[32,128,128]{2,1,0:T(8,128)S(1)} %fusion.47), kind=kCustom, calls=%fused_computation.6.clone.1 | custom fusion | flops 524288 | bytes 6291584 | tf_op jit(solution)/shard_map/while/body/eval_jaxpr/scatter-add | solution.py:64
  173.2 0.1 constant_dynamic-slice_fusion.5
  173.3 2.8 gather_fusion.1
  176.1 2.1 fusion.47
  178.3 6.5 %scatter_fusion.1 = f32[128,28,128]{2,0,1:T(8,128)} fusion(f32[128,28,128]{2,0,1:T(8,128)} %get-tuple-element.359, s32[32]{0:T(128)S(1)} %get-tuple-element.320, f32[32,128,128]{2,1,0:T(8,128)S(1)} %fusion.47), kind=kCustom, calls=%fused_computation.6.clone.1 | custom fusion | flops 524288 | bytes 6291584 | tf_op jit(solution)/shard_map/while/body/eval_jaxpr/scatter-add | solution.py:64
  184.7 0.1 constant_dynamic-slice_fusion.5
  184.8 2.8 gather_fusion.1
  187.6 2.1 fusion.47
  189.8 6.3 %scatter_fusion.1 = f32[128,28,128]{2,0,1:T(8,128)} fusion(f32[128,28,128]{2,0,1:T(8,128)} %get-tuple-element.359, s32[32]{0:T(128)S(1)} %get-tuple-element.320, f32[32,128,128]{2,1,0:T(8,128)S(1)} %fusion.47), kind=kCustom, calls=%fused_computation.6.clone.1 | custom fusion | flops 524288 | bytes 6291584 | tf_op jit(solution)/shard_map/while/body/eval_jaxpr/scatter-add | solution.py:64
  196.1 0.1 constant_dynamic-slice_fusion.5
  196.1 2.9 gather_fusion.1
  199.1 2.1 fusion.47
  201.2 6.3 %scatter_fusion.1 = f32[128,28,128]{2,0,1:T(8,128)} fusion(f32[128,28,128]{2,0,1:T(8,128)} %get-tuple-element.359, s32[32]{0:T(128)S(1)} %get-tuple-element.320, f32[32,128,128]{2,1,0:T(8,128)S(1)} %fusion.47), kind=kCustom, calls=%fused_computation.6.clone.1 | custom fusion | flops 524288 | bytes 6291584 | tf_op jit(solution)/shard_map/while/body/eval_jaxpr/scatter-add | solution.py:64
  207.5 1.6 convert_element_type.17
  209.1 0.6 copy.37
  209.8 0.5 reshape.37
  210.3 0.6 gather_fusion.2
  210.9 0.2 broadcast_select_fusion
  211.0 1.3 collective-permute-start
  212.3 172.1 %reduce-scatter.2.cloned.1.call-done = f32[4,128,128]{2,1,0:T(8,128)} async-done(((f32[128,128,128]{2,1,0:T(8,128)}), f32[4,128,128]{2,1,0:T(8,128)}) %reduce-scatter.2.cloned.1.call-update) | async-done | bytes 262160 | tf_op jit(solution)/shard_map/reduce_scatter | solution.py:78
  384.5 51.2 %all-reduce.2.cloned.1.call-done = f32[4,128,128]{2,1,0:T(8,128)} async-done(((f32[4,128,128]{2,1,0:T(8,128)}), f32[4,128,128]{2,1,0:T(8,128)}) %all-reduce.2.cloned.1.call-update) | async-done | bytes 262160 | tf_op jit(solution)/shard_map/psum | solution.py:84
  435.7 1.7 multiply_bitcast_fusion
  437.3 0.9 copy.61
  (32 shorter events, 0.3 us)
Async XLA Ops:
  7.2 86.3 %all-gather.4.cloned.1.call-start = ((), (), s32[]{:S(2)}) async-start(), calls=%async_computation.3 | async-start | bytes 4325376 | tf_op jit(solution)/shard_map/all_gather | solution.py:68
  7.9 376.5 %reduce-scatter.2.cloned.1.call-start = ((), (), s32[]{:S(2)}) async-start(), calls=%async_computation.1 | async-start | bytes 8650752 | tf_op jit(solution)/shard_map/reduce_scatter | solution.py:78
  159.6 0.7 copy-start
  159.7 276.0 %all-reduce.2.cloned.1.call-start = ((), (), s32[]{:S(2)}) async-start(), calls=%async_computation.2 | async-start | bytes 524288 | tf_op jit(solution)/shard_map/psum | solution.py:84
  211.0 173.4 %collective-permute-start = (bf16[4,32,3584]{2,1,0:T(8,128)(2,1)S(1)}, bf16[4,32,3584]{2,1,0:T(8,128)(2,1)S(1)}, u32[]{:S(2)}, u32[]{:S(2)}) collective-permute-start(bf16[4,32,3584]{2,1,0:T(8,128)(2,1)S(1)} %broadcast_select_fusion), channel_id=1, source_target_pairs={{128,0},{129,1},{130,2},{131,3},{132,4},{133,5},{134,6},{135,7},{1... | collective-permute-start | bytes 2752520 | tf_op jit(solution)/shard_map/ppermute | solution.py:11
Sparse Core Ops, SparseCore 0:
  10.6 82.8 all-gather.3
  159.8 224.6 reduce-scatter.1
  387.3 48.3 all-reduce.1
where the time goes:
time: 447 us; the launch traced here: 445 us
  waiting for transfers between devices  257 us (57%)
  other arithmetic  62.9 us (14%)
  local copies, waits for them, and re-layouts  43.9 us (10%)
  blocking collectives  40.7 us (9%)
  matrix products  25.1 us (6%)
  between operations  13.8 us (3%)
    reduce_scatter x1, waiting for transfers between devices, local(): lax.psum_scatter(jnp.einsum('tbk,tbn->bkn', rows_in, cols_in, preferred_e...  172 us
    psum x1, waiting for transfers between devices, local(): summed = lax.psum(owned_grads, 'dp')  51.2 us
    all_gather x1, blocking collectives, local(): all_indices = lax.all_gather(pattern[0], 'fsdp', axis=0, tiled=True)  40.7 us
    all_gather x1, waiting for transfers between devices, local(): lax.all_gather(own_blocks, 'fsdp', axis=0, tiled=True)  32.7 us
    scatter-add x4, other arithmetic, backward_step(): return running.at[:, indices[:, 0]].add(product)  25.5 us
    scatter-add x4, other arithmetic, forward_step(): return running.at[:, indices[:, 1]].add(product)  24.8 us
    gather x4, local copies, waits for them, and re-layouts, backward_step(): cols_in = jnp.take(grad_cols, indices[:, 1], axis=1)  11.3 us
  transfers between devices with their start and end apart: 4, of which 3 were waited for; matrix products, arithmetic and copies ran while one was open for 14% of the time, Pallas kernels for 0%

commit v1 on v0

--- a/solution.py
+++ b/solution.py
@@ -1,8 +1,19 @@
+import functools
 import math
 import jax
 import jax.numpy as jnp
 from jax import lax
 from jax.sharding import PartitionSpec as P
+
+
+def time_tails_all(v0, in_dim):
+    heard = jnp.concatenate(
+        lax.all_to_all(jnp.stack([v0] * lax.axis_size("fsdp")), "fsdp", 0, 0), axis=in_dim
+    )
+    return heard
+
+
+perform_the_state = functools.partial(time_tails_all, in_dim=0)
 
 
 def passed_along(block, axis, distance):
@@ -64,9 +75,7 @@
         return running.at[:, indices[:, 0]].add(product)
 
     back_zero = jnp.zeros((tok_rows, row_count, block_size), jnp.float32)
-    input_grad = in_groups(
-        backward_step, back_zero, lax.all_gather(own_blocks, "fsdp", axis=0, tiled=True)
-    )
+    input_grad = in_groups(backward_step, back_zero, perform_the_state(own_blocks))
     input_grad = input_grad.astype(jnp.bfloat16).reshape(
         micro_count, activations.shape[2], activations.shape[3]
     )

time: 447 us -> 489 us (1.094)
  waiting for transfers between devices: 257 us -> 285 us
  local copies, waits for them, and re-layouts: 43.9 us -> 51 us
  starting transfers between devices: 1.59 us -> 7.47 us
    all_to_all x0 -> x1, waiting for transfers between devices: none -> 118 us  [time_tails_all(): lax.all_to_all(jnp.stack([v0] * lax.axis_size('fsdp')), 'fsdp', 0, 0)]
    reduce_scatter x1, waiting for transfers between devices: 172 us -> 82.3 us  [local(): lax.psum_scatter(jnp.einsum('tbk,tbn->bkn', rows_in, cols_in, preferred_e...]
    all_to_all x0 -> x1, starting transfers between devices: none -> 5.88 us  [time_tails_all(): lax.all_to_all(jnp.stack([v0] * lax.axis_size('fsdp')), 'fsdp', 0, 0)]
  transfers between devices with their start and end apart: 4 -> 5, of which waited for: 3 -> 4; matrix products, arithmetic and copies ran while one was open for 14% -> 15% of each run, Pallas kernels for 0% -> 0%
where the time goes in v1:
time: 489 us; the launch traced here: 487 us
  waiting for transfers between devices  285 us (58%)
  other arithmetic  62.9 us (13%)
  local copies, waits for them, and re-layouts  51 us (10%)
  blocking collectives  40.7 us (8%)
  matrix products  26.4 us (5%)
  between operations  13.9 us (3%)
  starting transfers between devices  7.47 us (2%)
    all_to_all x1, waiting for transfers between devices, time_tails_all(): lax.all_to_all(jnp.stack([v0] * lax.axis_size('fsdp')), 'fsdp', 0, 0)  118 us
    reduce_scatter x1, waiting for transfers between devices, local(): lax.psum_scatter(jnp.einsum('tbk,tbn->bkn', rows_in, cols_in, preferred_e...  82.3 us
    psum x1, waiting for transfers between devices, local(): summed = lax.psum(owned_grads, 'dp')  51.3 us
    all_gather x1, blocking collectives, local(): all_indices = lax.all_gather(pattern[0], 'fsdp', axis=0, tiled=True)  40.7 us
    all_gather x1, waiting for transfers between devices, local(): lax.all_gather(own_blocks, 'fsdp', axis=0, tiled=True)  32.7 us
    scatter-add x4, other arithmetic, backward_step(): return running.at[:, indices[:, 0]].add(product)  25.6 us
    scatter-add x4, other arithmetic, forward_step(): return running.at[:, indices[:, 1]].add(product)  24.8 us
    gather x4, local copies, waits for them, and re-layouts, backward_step(): cols_in = jnp.take(grad_cols, indices[:, 1], axis=1)  14.9 us
  transfers between devices with their start and end apart: 5, of which 4 were waited for; matrix products, arithmetic and copies ran while one was open for 15% of the time, Pallas kernels for 0%

profile of v1, /device:TPU:1, one launch (start us, length us, event | category | flops | bytes accessed | tf_op | source)
XLA Modules:
  0.0 487.2 jit_solution(17720586900554729488)
XLA Ops:
  7.2 0.7 all-gather.4.cloned.1.call-update
  7.9 0.8 copy.31
  8.7 40.7 %all-gather = s32[1,128,2]{2,0,1:T(1,128)S(1)} all-gather(s32[1,4,2]{2,0,1:T(1,128)S(1)} %copy.31), channel_id=2, replica_groups=mesh['section'=2,'fsdp'=32,'dp'=4] {'fsdp'}, dimensions={1}, use_global_device_ids=true | all-gather | bytes 1056 | tf_op jit(solution)/shard_map/all_gather | solution.py:50
  49.5 1.6 reshape_squeeze.4
  51.1 0.4 copy.34
  51.5 5.9 %copy.41 = f32[16,8,112,128]{3,2,1,0:T(8,128)} copy(bf16[16,8,112,128]{3,1,2,0:T(8,128)(2,1)} %bitcast.53) | data formatting | bytes 11010048
  57.3 0.2 fusion.29
  57.5 3.1 gather_fusion.3
  60.6 0.2 and_reduce_fusion.1
  60.8 32.7 %all-gather.4.cloned.1.call-done = bf16[1,128,128,128]{3,2,0,1:T(8,128)(2,1)} async-done(((bf16[1,4,128,128]{3,2,0,1:T(8,128)(2,1)}), bf16[1,128,128,128]{3,2,0,1:T(8,128)(2,1)}) %all-gather.4.cloned.1.call-update) | async-done | bytes 4194320 | tf_op jit(solution)/shard_map/all_gather | solution.py:62
  93.5 3.9 broadcast_in_dim.90
  97.5 40.1 %while.26 = (s32[]{:T(128)}, f32[128,112,128]{2,0,1:T(8,128)}, s32[128,2]{0,1:T(2,128)S(1)}, bf16[128,128,128]{2,1,0:T(8,128)(2,1)}, bf16[128,28,128]{2,0,1:T(8,...) while((s32[]{:T(128)}, f32[128,112,128]{2,0,1:T(8,128)}, s32[128,2]{0,1:T(2,128)S(1)}, ...), condition=%wide.region_2.3_spmd, body=%wide.region_0.2_spmd.sunk | while | flops 135267712 | bytes 12588755 | solution.py:38
  97.5 0.1 constant_dynamic-slice_fusion.4
  97.5 1.7 gather_fusion
  99.2 2.0 fusion.43
  101.3 6.2 %scatter_fusion = f32[128,112,128]{2,0,1:T(8,128)} fusion(f32[128,112,128]{2,0,1:T(8,128)} %get-tuple-element.332, s32[32]{0:T(128)S(1)} %get-tuple-element.313, f32[32,128,128]{2,1,0:T(8,128)S(1)} %fusion.43), kind=kCustom, calls=%fused_computation.5.clone.1 | custom fusion | flops 524288 | bytes 6291584 | tf_op jit(solution)/shard_map/while/body/eval_jaxpr/scatter-add | solution.py:58
  107.5 0.1 constant_dynamic-slice_fusion.4
  107.6 1.7 gather_fusion
  109.3 2.0 fusion.43
  111.3 6.2 %scatter_fusion = f32[128,112,128]{2,0,1:T(8,128)} fusion(f32[128,112,128]{2,0,1:T(8,128)} %get-tuple-element.332, s32[32]{0:T(128)S(1)} %get-tuple-element.313, f32[32,128,128]{2,1,0:T(8,128)S(1)} %fusion.43), kind=kCustom, calls=%fused_computation.5.clone.1 | custom fusion | flops 524288 | bytes 6291584 | tf_op jit(solution)/shard_map/while/body/eval_jaxpr/scatter-add | solution.py:58
  117.5 0.1 constant_dynamic-slice_fusion.4
  117.6 1.7 gather_fusion
  119.3 2.0 fusion.43
  121.3 6.2 %scatter_fusion = f32[128,112,128]{2,0,1:T(8,128)} fusion(f32[128,112,128]{2,0,1:T(8,128)} %get-tuple-element.332, s32[32]{0:T(128)S(1)} %get-tuple-element.313, f32[32,128,128]{2,1,0:T(8,128)S(1)} %fusion.43), kind=kCustom, calls=%fused_computation.5.clone.1 | custom fusion | flops 524288 | bytes 6291584 | tf_op jit(solution)/shard_map/while/body/eval_jaxpr/scatter-add | solution.py:58
  127.5 0.1 constant_dynamic-slice_fusion.4
  127.6 1.7 gather_fusion
  129.3 2.0 fusion.43
  131.3 6.2 %scatter_fusion = f32[128,112,128]{2,0,1:T(8,128)} fusion(f32[128,112,128]{2,0,1:T(8,128)} %get-tuple-element.332, s32[32]{0:T(128)S(1)} %get-tuple-element.313, f32[32,128,128]{2,1,0:T(8,128)S(1)} %fusion.43), kind=kCustom, calls=%fused_computation.5.clone.1 | custom fusion | flops 524288 | bytes 6291584 | tf_op jit(solution)/shard_map/while/body/eval_jaxpr/scatter-add | solution.py:58
  137.5 8.4 %fusion.20 = bf16[128,112,128]{2,0,1:T(8,128)(2,1)} fusion(f32[128,112,128]{2,1,0:T(8,128)} %bitcast.51, f32[128,112,128]{2,0,1:T(8,128)} %get-tuple-element.190), kind=kLoop, calls=%fused_computation.38 | loop fusion | flops 16515072 | bytes 18350080 | tf_op jit(solution)/shard_map/convert_element_type | solution.py:64
  146.0 5.1 %gather_fusion.4 = bf16[128,128,128]{2,1,0:T(8,128)(2,1)} fusion(bf16[128,112,128]{2,0,1:T(8,128)(2,1)} %fusion.20, s32[1024]{0:T(1024)S(1)} %get-tuple-element.250), kind=kCustom, calls=%fused_computation.4 | custom fusion | bytes 8389120 | tf_op jit(solution)/shard_map/jit(_take)/gather | solution.py:86
  151.1 8.5 %fusion.21 = f32[128,128,128]{2,1,0:T(8,128)} fusion(bf16[128,128,128]{2,1,0:T(8,128)(2,1)} %gather_fusion.4, bf16[128,128,128]{2,1,0:T(8,128)(2,1)} %gather_fusion.3, pred[128]{0:T(512)(128)(4,1)S(1)} %get-tuple-element.223, pred[128]{0:T(512)(128)(4,1)S(1)} %get-tuple-element.222), kind=kOutput, calls=%fused_computation.39 | convolution fusion | flops 541065216 | bytes 16777472 | tf_op jit(solution)/shard_map/tbk,tbn->bkn/dot_general | solution.py:88
  159.6 0.9 copy-done
  160.5 3.0 stack.3
  163.5 5.9 %all-to-all-start = ((bf16[32,4,128,128]{3,2,1,0:T(8,128)(2,1)}), bf16[32,4,128,128]{3,2,1,0:T(8,128)(2,1)}, u32[]{:S(2)}, u32[]{:S(2)}) async-start(bf16[32,4,128,128]{3,2,1,0:T(8,128)(2,1)} %stack.3), calls=%async_computation | async-start | bytes 8388608 | tf_op jit(solution)/shard_map/all_to_all | solution.py:11
  169.4 0.2 all-reduce.2.cloned.1.call-start
  169.6 117.8 %all-to-all-done = bf16[32,4,128,128]{3,2,1,0:T(8,128)(2,1)} async-done(((bf16[32,4,128,128]{3,2,1,0:T(8,128)(2,1)}), bf16[32,4,128,128]{3,2,1,0:T(8,128)(2,1)}, u32[]{:S(2)}, u32[]{:S(2)}) %all-to-all-start) | async-done | bytes 4194336 | tf_op jit(solution)/shard_map/all_to_all | solution.py:11
  287.5 1.5 broadcast_in_dim.89
  289.0 50.6 %while.27 = (s32[]{:T(128)}, f32[128,28,128]{2,0,1:T(8,128)}, s32[128,2]{0,1:T(2,128)S(1)}, bf16[128,128,128]{2,1,0:T(8,128)(2,1)}, bf16[128,112,128]{2,0,1:T(8,...) while((s32[]{:T(128)}, f32[128,28,128]{2,0,1:T(8,128)}, s32[128,2]{0,1:T(2,128)S(1)}, ...), condition=%wide.region_5.6_spmd, body=%wide.region_3.5_spmd.sunk | while | flops 135267712 | bytes 12588755 | solution.py:38
  289.0 0.1 constant_dynamic-slice_fusion.5
  289.1 3.7 gather_fusion.1
  292.8 2.4 fusion.47
  295.2 6.5 %scatter_fusion.1 = f32[128,28,128]{2,0,1:T(8,128)} fusion(f32[128,28,128]{2,0,1:T(8,128)} %get-tuple-element.359, s32[32]{0:T(128)S(1)} %get-tuple-element.320, f32[32,128,128]{2,1,0:T(8,128)S(1)} %fusion.47), kind=kCustom, calls=%fused_computation.6.clone.1 | custom fusion | flops 524288 | bytes 6291584 | tf_op jit(solution)/shard_map/while/body/eval_jaxpr/scatter-add | solution.py:75
  301.7 0.1 constant_dynamic-slice_fusion.5
  301.8 3.7 gather_fusion.1
  305.5 2.4 fusion.47
  308.0 6.2 %scatter_fusion.1 = f32[128,28,128]{2,0,1:T(8,128)} fusion(f32[128,28,128]{2,0,1:T(8,128)} %get-tuple-element.359, s32[32]{0:T(128)S(1)} %get-tuple-element.320, f32[32,128,128]{2,1,0:T(8,128)S(1)} %fusion.47), kind=kCustom, calls=%fused_computation.6.clone.1 | custom fusion | flops 524288 | bytes 6291584 | tf_op jit(solution)/shard_map/while/body/eval_jaxpr/scatter-add | solution.py:75
  314.2 0.1 constant_dynamic-slice_fusion.5
  314.3 3.8 gather_fusion.1
  318.0 2.4 fusion.47
  320.5 6.5 %scatter_fusion.1 = f32[128,28,128]{2,0,1:T(8,128)} fusion(f32[128,28,128]{2,0,1:T(8,128)} %get-tuple-element.359, s32[32]{0:T(128)S(1)} %get-tuple-element.320, f32[32,128,128]{2,1,0:T(8,128)S(1)} %fusion.47), kind=kCustom, calls=%fused_computation.6.clone.1 | custom fusion | flops 524288 | bytes 6291584 | tf_op jit(solution)/shard_map/while/body/eval_jaxpr/scatter-add | solution.py:75
  327.0 0.1 constant_dynamic-slice_fusion.5
  327.1 3.7 gather_fusion.1
  330.8 2.4 fusion.47
  333.2 6.4 %scatter_fusion.1 = f32[128,28,128]{2,0,1:T(8,128)} fusion(f32[128,28,128]{2,0,1:T(8,128)} %get-tuple-element.359, s32[32]{0:T(128)S(1)} %get-tuple-element.320, f32[32,128,128]{2,1,0:T(8,128)S(1)} %fusion.47), kind=kCustom, calls=%fused_computation.6.clone.1 | custom fusion | flops 524288 | bytes 6291584 | tf_op jit(solution)/shard_map/while/body/eval_jaxpr/scatter-add | solution.py:75
  339.6 1.7 convert_element_type.17
  341.2 0.6 copy.37
  341.9 0.5 reshape.42
  342.3 0.6 gather_fusion.2
  343.0 0.2 broadcast_select_fusion
  343.1 1.3 collective-permute-start
  344.4 82.3 %reduce-scatter.2.cloned.1.call-done = f32[4,128,128]{2,1,0:T(8,128)} async-done(((f32[128,128,128]{2,1,0:T(8,128)}), f32[4,128,128]{2,1,0:T(8,128)}) %reduce-scatter.2.cloned.1.call-update) | async-done | bytes 262160 | tf_op jit(solution)/shard_map/reduce_scatter | solution.py:87
  426.8 51.3 %all-reduce.2.cloned.1.call-done = f32[4,128,128]{2,1,0:T(8,128)} async-done(((f32[4,128,128]{2,1,0:T(8,128)}), f32[4,128,128]{2,1,0:T(8,128)}) %all-reduce.2.cloned.1.call-update) | async-done | bytes 262160 | tf_op jit(solution)/shard_map/psum | solution.py:93
  478.1 1.7 multiply_bitcast_fusion
  479.8 0.9 copy.61
  (37 shorter events, 0.4 us)
Async XLA Ops:
  7.2 86.3 %all-gather.4.cloned.1.call-start = ((), (), s32[]{:S(2)}) async-start(), calls=%async_computation.4 | async-start | bytes 4325376 | tf_op jit(solution)/shard_map/all_gather | solution.py:62
  7.9 418.9 %reduce-scatter.2.cloned.1.call-start = ((), (), s32[]{:S(2)}) async-start(), calls=%async_computation.2 | async-start | bytes 8650752 | tf_op jit(solution)/shard_map/reduce_scatter | solution.py:87
  159.6 0.9 copy-start
  163.5 6.1 %copy-start.1 = (s32[4]{0:T(128)S(1)}, s32[4]{0:T(128)}, u32[]{:S(2)}) copy-start(s32[4]{0:T(128)} %param.13) | copy-start | bytes 52
  163.5 124.0 %all-to-all-start = ((bf16[32,4,128,128]{3,2,1,0:T(8,128)(2,1)}), bf16[32,4,128,128]{3,2,1,0:T(8,128)(2,1)}, u32[]{:S(2)}, u32[]{:S(2)}) async-start(bf16[32,4,128,128]{3,2,1,0:T(8,128)(2,1)} %stack.3), calls=%async_computation | async-start | bytes 8388608 | tf_op jit(solution)/shard_map/all_to_all | solution.py:11
  169.4 308.7 %all-reduce.2.cloned.1.call-start = ((), (), s32[]{:S(2)}) async-start(), calls=%async_computation.3 | async-start | bytes 524288 | tf_op jit(solution)/shard_map/psum | solution.py:93
  343.1 83.7 %collective-permute-start = (bf16[4,32,3584]{2,1,0:T(8,128)(2,1)S(1)}, bf16[4,32,3584]{2,1,0:T(8,128)(2,1)S(1)}, u32[]{:S(2)}, u32[]{:S(2)}) collective-permute-start(bf16[4,32,3584]{2,1,0:T(8,128)(2,1)S(1)} %broadcast_select_fusion), channel_id=1, source_target_pairs={{128,0},{129,1},{130,2},{131,3},{132,4},{133,5},{134,6},{135,7},{1... | collective-permute-start | bytes 2752520 | tf_op jit(solution)/shard_map/ppermute | solution.py:22
Sparse Core Ops, SparseCore 0:
  10.6 82.8 all-gather.3
  159.7 266.9 reduce-scatter.1
  429.6 48.4 all-reduce.1
